TPU v7x, 256 devices: a whole 4x4x8 slice. The times are simulated.
256 devices in a mesh: fsdp: 16 (over x_lo, z), factor: 16 (over x_hi, y, core).
Axes of the slice: x: 4 (x_hi: 2, x_lo: 2; x = x_hi * 2 + x_lo), y: 4, z: 8, core: 2. Of those that a mesh axis runs over, the one named last changes fastest.
Arguments:
- activations: bfloat16 [256, 16, 16, 512], P(('fsdp', 'factor')), may hold values from -12 to 12
- cotangent: bfloat16 [256, 16, 16, 512], P(('fsdp', 'factor')), may hold values from -0.23632812 to 0.23632812
- weight: bfloat16 [4608, 512], P('fsdp'), may hold values from -0.09375 to 0.09375
- a_factor_old: float32 [4608, 4608], P('factor', 'fsdp'), may hold values from -0.11785113 to 5, as said below
- g_factor_old: float32 [512, 512], P('factor'), may hold values from -0.35355339 to 5, as said below
- a_inverse: float32 [4608, 4608], P('fsdp', 'factor'), may hold values from -0.09375 to 0.09375
- g_inverse: float32 [512, 512], replicated, may hold values from -0.25 to 0.25
Outputs:
- conv_out: bfloat16 [256, 16, 16, 512], P(('fsdp', 'factor'))
- a_factor: float32 [4608, 4608], P('factor', 'fsdp')
- g_factor: float32 [512, 512], P('factor')
- natural_grad: bfloat16 [4608, 512], P('fsdp', 'factor')
Inputs may be any that keep to these rules, and one draw needn't show every extreme that they name: `a_factor_old`: a symmetric matrix. `g_factor_old`: a symmetric matrix.
All inputs are finite; a program needn't handle non-finite values.
Results may differ from a plain program's by a relative error of at most 0.0017.
Values may be sent and summed in bfloat16 or wider, within the bound.
A program may use at most 192 MiB of HBM per device.

v0:
```python
import jax
import jax.numpy as jnp
from jax import lax
from jax.sharding import PartitionSpec as P


def unfold(images):
    side = images.shape[1]
    padded = jnp.pad(images, ((0, 0), (1, 1), (1, 1), (0, 0)))
    tap_list = [
        padded[:, row_off : row_off + side, col_off : col_off + side, :]
        for row_off in range(3)
        for col_off in range(3)
    ]
    return jnp.concatenate(tap_list, axis=3).reshape(-1, 9 * images.shape[3])


def contract(first_op, second_op):
    return lax.dot_general(
        first_op, second_op, (((0,), (0,)), ((), ())), preferred_element_type=jnp.float32
    )


def per_device(activations, cotangent, weight, a_factor_old, g_factor_old, a_inverse, g_inverse):
    channels = activations.shape[3]
    own_patches = unfold(activations)
    own_cot = cotangent.reshape(-1, channels)
    factor_index = lax.axis_index("factor")
    rows_per = a_factor_old.shape[0]
    row_start = factor_index * rows_per
    conv_total = jnp.dot(
        own_patches,
        lax.all_gather(weight, "fsdp", axis=0, tiled=True),
        preferred_element_type=jnp.float32,
    )
    conv_out = conv_total.astype(jnp.bfloat16).reshape(activations.shape)
    patches = unfold(lax.all_gather(activations, "factor", axis=0, tiled=True))
    a_partial = contract(lax.dynamic_slice_in_dim(patches, row_start, rows_per, 1), patches)
    grad_partial = lax.psum_scatter(
        contract(own_patches, own_cot), "factor", scatter_dimension=0, tiled=True
    )
    a_summed = lax.psum_scatter(a_partial, "fsdp", scatter_dimension=1, tiled=True)
    pixel_total = float(
        activations.shape[1]
        * activations.shape[2]
        * lax.axis_size("fsdp")
        * lax.axis_size("factor")
    )
    a_factor = 0.5 * a_factor_old + 0.5 * (a_summed / pixel_total)
    grad_rows = lax.psum(grad_partial, "fsdp")
    g_partial = contract(own_cot, own_cot)
    g_rows_count = g_factor_old.shape[0]
    g_summed = lax.psum(g_partial, ("fsdp", "factor"))
    g_rows = lax.dynamic_slice_in_dim(g_summed, factor_index * g_rows_count, g_rows_count, 0)
    g_factor = 0.5 * g_factor_old + 0.5 * g_rows
    mixed = jnp.dot(
        grad_rows, g_inverse, precision=lax.Precision.HIGHEST, preferred_element_type=jnp.float32
    )
    partial_rows = jnp.dot(
        a_inverse, mixed, precision=lax.Precision.HIGHEST, preferred_element_type=jnp.float32
    )
    summed_rows = lax.psum(partial_rows, "factor")
    tile_width = channels // lax.axis_size("factor")
    result_tile = lax.dynamic_slice_in_dim(summed_rows, factor_index * tile_width, tile_width, 1)
    return (conv_out, a_factor, g_factor, result_tile.astype(jnp.bfloat16))


def solution(mesh):
    return jax.shard_map(
        per_device,
        mesh=mesh,
        in_specs=(
            P(("fsdp", "factor"), None, None, None),
            P(("fsdp", "factor"), None, None, None),
            P("fsdp", None),
            P("factor", "fsdp"),
            P("factor", None),
            P("fsdp", "factor"),
            P(),
        ),
        out_specs=(
            P(("fsdp", "factor"), None, None, None),
            P("factor", "fsdp"),
            P("factor", None),
            P("fsdp", "factor"),
        ),
        check_vma=False,
    )
```

profile of v0, /device:TPU:0, one launch (start us, length us, event | category | flops | bytes accessed | tf_op | source)
XLA Modules:
  0.0 599.1 jit_solution(16298183459508021695)
XLA Ops:
  8.0 0.0 copy-start
  8.0 0.0 all-gather.5.cloned.1.call-start
  8.1 0.7 all-gather.5.cloned.1.call-update
  8.8 0.0 reduce-scatter.5.cloned.1.call-start
  8.8 1.0 fusion.10
  9.8 1.0 fusion.11
  10.8 1.0 fusion.12
  11.8 1.0 fusion.13
  12.8 1.0 constant_dynamic-update-slice_fusion
  13.8 1.0 fusion.14
  14.8 1.0 fusion.15
  15.9 1.0 fusion.16
  16.8 0.1 fusion.17
  16.9 1.4 copy-done.6
  18.3 5.1 convolution_bitcast_fusion
  23.4 0.0 reduce-scatter.5.cloned.1.call-update
  23.4 0.0 all-reduce.6.cloned.1.call-start
  23.4 1.3 convolution_bitcast_fusion.2
  24.8 0.0 all-reduce.6.cloned.1.call-update
  24.8 0.0 all-gather.3.cloned.1.call-start
  24.8 0.7 all-gather.3.cloned.1.call-update
  25.5 0.2 all-reduce.8.cloned.1.call-start
  25.8 47.5 %all-gather.5.cloned.1.call-done = bf16[16,16,16,512]{3,2,1,0:T(8,128)(2,1)} async-done(((bf16[1,16,16,512]{3,2,1,0:T(8,128)(2,1)}), bf16[16,16,16,512]{3,2,1,0:T(8,128)(2,1)}) %all-gather.5.cloned.1.call-update) | async-done | bytes 4194320 | tf_op jit(solution)/shard_map/all_gather | solution.py:37
  73.3 5.6 fusion
  78.9 2.7 fusion.1
  81.6 4.1 fusion.2
  85.6 4.2 fusion.3
  89.9 2.8 constant_dynamic-update-slice_fusion.1
  92.6 4.2 fusion.4
  96.9 4.1 fusion.5
  100.9 2.7 fusion.6
  103.7 4.2 fusion.7
  107.9 82.9 %reduce-scatter.5.cloned.1.call-done = f32[288,512]{1,0:T(8,128)} async-done(((f32[4608,512]{1,0:T(8,128)}), f32[288,512]{1,0:T(8,128)}) %reduce-scatter.5.cloned.1.call-update) | async-done | bytes 589840 | tf_op jit(solution)/shard_map/reduce_scatter | solution.py:39
  190.8 0.0 all-reduce.8.cloned.1.call-update
  190.9 0.0 reduce-scatter.7.cloned.1.call-start
  190.9 27.4 %convolution_bitcast_fusion.1 = f32[4608,288]{1,0:T(8,128)} fusion(bf16[4096,4608]{1,0:T(8,128)(2,1)} %bitcast.27, s32[]{:T(128)S(6)} %select_n.7), kind=kOutput, calls=%fused_computation.9 | convolution fusion | flops 10871635968 | bytes 46202884
  218.3 0.0 reduce-scatter.7.cloned.1.call-update
  218.4 91.2 %all-reduce.6.cloned.1.call-done = f32[512,512]{1,0:T(8,128)} async-done(((f32[512,512]{1,0:T(8,128)}), f32[512,512]{1,0:T(8,128)}) %all-reduce.6.cloned.1.call-update) | async-done | bytes 1048592 | tf_op jit(solution)/shard_map/psum | solution.py:53
  309.5 1.5 add_multiply_fusion
  311.0 5.2 convolution_convert_fusion
  316.2 130.5 %all-reduce.8.cloned.1.call-done = f32[288,512]{1,0:T(8,128)} async-done(((f32[288,512]{1,0:T(8,128)}), f32[288,512]{1,0:T(8,128)}) %all-reduce.8.cloned.1.call-update) | async-done | bytes 589840 | tf_op jit(solution)/shard_map/psum | solution.py:50
  446.8 2.2 fusion.21
  449.0 1.1 convolution_bitcast_fusion.3
  450.1 138.8 %all-reduce.9 = bf16[288,512]{1,0:T(8,128)(2,1)S(1)} all-reduce(f32[288,512]{1,0:T(8,128)S(1)} %convolution_bitcast_fusion.3), channel_id=1, replica_groups=mesh['fsdp'=16,'factor'=16] {'factor'}, use_global_device_ids=true, to_apply=%region_4.5 | all-reduce | flops 147456 | bytes 884736 | tf_op jit(solution)/shard_map/psum | solution.py:62
  589.0 0.1 dynamic-slice_convert_fusion
  589.1 0.7 copy.12
  589.8 1.2 copy.14
  591.0 0.8 multiply_add_fusion
  (16 shorter events, 0.0 us)
Async XLA Ops:
  8.0 438.8 %copy-start = (f32[512,512]{1,0:T(8,128)S(1)}, f32[512,512]{1,0:T(8,128)}, u32[]{:S(2)}) copy-start(f32[512,512]{1,0:T(8,128)} %param.13) | copy-start | bytes 3145732
  8.0 8.8 %copy-start.2 = (bf16[1,16,16,512]{3,2,1,0:T(8,128)(2,1)S(1)}, bf16[1,16,16,512]{3,2,1,0:T(8,128)(2,1)}, u32[]{:S(2)}) copy-start(bf16[1,16,16,512]{3,2,1,0:T(8,128)(2,1)} %param.7) | copy-start | bytes 786436
  8.0 10.3 %copy-start.7 = (bf16[1,16,16,512]{3,2,1,0:T(8,128)(2,1)S(1)}, bf16[1,16,16,512]{3,2,1,0:T(8,128)(2,1)}, u32[]{:S(2)}) copy-start(bf16[1,16,16,512]{3,2,1,0:T(8,128)(2,1)} %param.8) | copy-start | bytes 786436
  8.0 65.3 %all-gather.5.cloned.1.call-start = ((), (), s32[]{:S(2)}) async-start(), calls=%async_computation.3 | async-start | bytes 4456448 | tf_op jit(solution)/shard_map/all_gather | solution.py:37
  8.8 182.1 %reduce-scatter.5.cloned.1.call-start = ((), (), s32[]{:S(2)}) async-start(), calls=%async_computation.5 | async-start | bytes 10027008 | tf_op jit(solution)/shard_map/reduce_scatter | solution.py:39
  16.9 1.4 copy-start.6
  23.4 286.2 %all-reduce.6.cloned.1.call-start = ((), (), s32[]{:S(2)}) async-start(), calls=%async_computation.4 | async-start | bytes 2097152 | tf_op jit(solution)/shard_map/psum | solution.py:53
  24.8 286.2 %all-gather.3.cloned.1.call-start = ((), (), s32[]{:S(2)}) async-start(), calls=%async_computation.2 | async-start | bytes 5013504 | tf_op jit(solution)/shard_map/all_gather | solution.py:33
  25.5 421.2 %all-reduce.8.cloned.1.call-start = ((), (), s32[]{:S(2)}) async-start(), calls=%async_computation.6 | async-start | bytes 1179648 | tf_op jit(solution)/shard_map/psum | solution.py:50
  73.3 5.6 copy-start.1
  190.9 398.9 %reduce-scatter.7.cloned.1.call-start = ((), (), s32[]{:S(2)}) async-start(), calls=%async_computation.7 | async-start | bytes 7520256
  218.3 91.2 %copy-start.5 = (f32[32,512]{1,0:T(8,128)S(1)}, f32[32,512]{1,0:T(8,128)}, u32[]{:S(2)}) copy-start(f32[32,512]{1,0:T(8,128)} %param.11) | copy-start | bytes 196612
  311.0 137.9 %copy-start.3 = (f32[288,288]{1,0:T(8,128)S(1)}, f32[288,288]{1,0:T(8,128)}, u32[]{:S(2)}) copy-start(f32[288,288]{1,0:T(8,128)} %param.12) | copy-start | bytes 995332
  316.2 274.8 %copy-start.4 = (f32[288,288]{1,0:T(8,128)S(1)}, f32[288,288]{1,0:T(8,128)}, u32[]{:S(2)}) copy-start(f32[288,288]{1,0:T(8,128)} %param.10) | copy-start | bytes 995332
Sparse Core Ops, SparseCore 0:
  11.6 61.6 all-gather.4
  77.9 112.8 reduce-scatter.4
  192.8 76.6 all-gather.2
Sparse Core Ops, SparseCore 1:
  30.2 279.3 all-reduce.5
  312.0 134.6 all-reduce.7
  449.4 88.0 reduce-scatter.6
where the time goes:
time: 600 us; the launch traced here: 599 us
  waiting for transfers between devices  354 us (59%)
  blocking collectives  139 us (23%)
  local copies, waits for them, and re-layouts  46 us (8%)
  matrix products  42.4 us (7%)
  between operations  15.6 us (3%)
    psum x1, blocking collectives, per_device(): summed_rows = lax.psum(partial_rows, 'factor')  139 us
    psum x1, waiting for transfers between devices, per_device(): grad_rows = lax.psum(grad_partial, 'fsdp')  131 us
    psum x1, waiting for transfers between devices, per_device(): g_summed = lax.psum(g_partial, ('fsdp', 'factor'))  91.2 us
    reduce_scatter x1, waiting for transfers between devices, per_device(): lax.psum_scatter(contract(own_patches, own_cot), 'factor', scatter_dimens...  82.9 us
    all_gather x1, waiting for transfers between devices, per_device(): patches = unfold(lax.all_gather(activations, 'factor', axis=0, tiled=True))  47.5 us
    unnamed x34, local copies, waits for them, and re-layouts  41.7 us
    unnamed x1, matrix products  27.4 us
  transfers between devices with their start and end apart: 6, of which 4 were waited for; matrix products, arithmetic and copies ran while one was open for 15% of the time, Pallas kernels for 0%

commit v1 on v0

--- a/solution.py
+++ b/solution.py
@@ -59,7 +59,7 @@
     partial_rows = jnp.dot(
         a_inverse, mixed, precision=lax.Precision.HIGHEST, preferred_element_type=jnp.float32
     )
-    summed_rows = lax.psum(partial_rows, "factor")
+    summed_rows = jnp.sum(lax.all_gather(partial_rows, "factor"), axis=0)
     tile_width = channels // lax.axis_size("factor")
     result_tile = lax.dynamic_slice_in_dim(summed_rows, factor_index * tile_width, tile_width, 1)
     return (conv_out, a_factor, g_factor, result_tile.astype(jnp.bfloat16))

time: 600 us -> 863 us (1.44)
  waiting for transfers between devices: 354 us -> 748 us
  blocking collectives: 139 us -> 0 us
    psum x1, waiting for transfers between devices: 91.2 us -> 254 us  [per_device(): g_summed = lax.psum(g_partial, ('fsdp', 'factor'))]
    psum x1 -> x0, blocking collectives: 139 us -> none  [per_device(): summed_rows = lax.psum(partial_rows, 'factor')]
    unnamed x7 -> x8, waiting for transfers between devices: 1.43 us -> 86.6 us
    all_gather x0 -> x1, waiting for transfers between devices: none -> 80.1 us  [per_device(): summed_rows = jnp.sum(lax.all_gather(partial_rows, 'factor'), axis=0)]
    all_gather x1, waiting for transfers between devices: 0.01 us -> 76.8 us  [per_device(): lax.all_gather(weight, 'fsdp', axis=0, tiled=True)]
    psum x1, waiting for transfers between devices: 131 us -> 74.8 us  [per_device(): grad_rows = lax.psum(grad_partial, 'fsdp')]
    reduce_scatter x1, waiting for transfers between devices: 82.9 us -> 115 us  [per_device(): lax.psum_scatter(contract(own_patches, own_cot), 'factor', scatter_dimens...]
    all_gather x1, waiting for transfers between devices: 47.5 us -> 60.1 us  [per_device(): patches = unfold(lax.all_gather(activations, 'factor', axis=0, tiled=True))]
  transfers between devices with their start and end apart: 6 -> 7, of which waited for: 4 -> 7; matrix products, arithmetic and copies ran while one was open for 15% -> 9% of each run, Pallas kernels for 0% -> 0%
where the time goes in v1:
time: 863 us; the launch traced here: 859 us
  waiting for transfers between devices  748 us (87%)
  local copies, waits for them, and re-layouts  46.1 us (5%)
  matrix products  43.2 us (5%)
  between operations  14.3 us (2%)
    psum x1, waiting for transfers between devices, per_device(): g_summed = lax.psum(g_partial, ('fsdp', 'factor'))  254 us
    reduce_scatter x1, waiting for transfers between devices, per_device(): lax.psum_scatter(contract(own_patches, own_cot), 'factor', scatter_dimens...  115 us
    unnamed x8, waiting for transfers between devices  86.6 us
    all_gather x1, waiting for transfers between devices, per_device(): summed_rows = jnp.sum(lax.all_gather(partial_rows, 'factor'), axis=0)  80.1 us
    all_gather x1, waiting for transfers between devices, per_device(): lax.all_gather(weight, 'fsdp', axis=0, tiled=True)  76.8 us
    psum x1, waiting for transfers between devices, per_device(): grad_rows = lax.psum(grad_partial, 'fsdp')  74.8 us
    all_gather x1, waiting for transfers between devices, per_device(): patches = unfold(lax.all_gather(activations, 'factor', axis=0, tiled=True))  60.1 us
    unnamed x34, local copies, waits for them, and re-layouts  41.7 us
  transfers between devices with their start and end apart: 7, of which 7 were waited for; matrix products, arithmetic and copies ran while one was open for 9% of the time, Pallas kernels for 0%

profile of v1, /device:TPU:0, one launch (start us, length us, event | category | flops | bytes accessed | tf_op | source)
XLA Modules:
  0.0 859.1 jit_solution(3756716947887698507)
XLA Ops:
  7.2 0.0 reduce-scatter.5.cloned.1.call-start
  7.2 1.1 fusion.10
  8.4 1.0 fusion.11
  9.3 1.0 fusion.12
  10.4 1.0 fusion.13
  11.4 1.0 constant_dynamic-update-slice_fusion
  12.4 1.0 fusion.14
  13.4 1.0 fusion.15
  14.4 1.0 fusion.16
  15.4 0.1 fusion.17
  15.5 1.4 copy-done.6
  16.8 5.1 convolution_bitcast_fusion
  21.9 0.0 reduce-scatter.5.cloned.1.call-update
  21.9 0.0 all-gather.7.cloned.1.call-start
  22.0 0.7 all-gather.7.cloned.1.call-update
  22.7 0.0 all-reduce.7.cloned.1.call-start
  22.7 115.2 %reduce-scatter.5.cloned.1.call-done = f32[288,512]{1,0:T(8,128)} async-done(((f32[4608,512]{1,0:T(8,128)}), f32[288,512]{1,0:T(8,128)}) %reduce-scatter.5.cloned.1.call-update) | async-done | bytes 589840 | tf_op jit(solution)/shard_map/reduce_scatter | solution.py:39
  138.0 0.0 all-reduce.5.cloned.1.call-start
  138.0 1.3 convolution_bitcast_fusion.2
  139.4 0.0 all-gather.5.cloned.1.call-start
  139.4 0.5 all-gather.5.cloned.1.call-update
  140.0 0.2 reduce-scatter.7.cloned.1.call-start
  140.2 60.1 %all-gather.7.cloned.1.call-done = bf16[16,16,16,512]{3,2,1,0:T(8,128)(2,1)} async-done(((bf16[1,16,16,512]{3,2,1,0:T(8,128)(2,1)}), bf16[16,16,16,512]{3,2,1,0:T(8,128)(2,1)}) %all-gather.7.cloned.1.call-update) | async-done | bytes 4194320 | tf_op jit(solution)/shard_map/all_gather | solution.py:37
  200.3 5.6 fusion
  205.9 2.7 fusion.1
  208.7 4.0 fusion.2
  212.7 4.2 fusion.3
  216.8 2.7 constant_dynamic-update-slice_fusion.1
  219.5 4.2 fusion.4
  223.7 4.1 fusion.5
  227.8 2.8 fusion.6
  230.6 4.3 fusion.7
  234.9 27.5 %convolution_bitcast_fusion.1 = f32[4608,288]{1,0:T(8,128)} fusion(bf16[4096,4608]{1,0:T(8,128)(2,1)} %bitcast.29, s32[]{:T(128)S(6)} %select_n.7), kind=kOutput, calls=%fused_computation.9 | convolution fusion | flops 10871635968 | bytes 46202884
  262.4 0.0 all-gather.9.cloned.1.call-start
  262.4 74.8 %all-reduce.7.cloned.1.call-done = f32[288,512]{1,0:T(8,128)} async-done(((f32[288,512]{1,0:T(8,128)}), f32[288,512]{1,0:T(8,128)}) %all-reduce.7.cloned.1.call-update) | async-done | bytes 589840 | tf_op jit(solution)/shard_map/psum | solution.py:50
  337.2 2.2 fusion.21
  339.4 2.0 convolution_bitcast_fusion.3
  341.4 254.3 %all-reduce.5.cloned.1.call-done = f32[512,512]{1,0:T(8,128)} async-done(((f32[512,512]{1,0:T(8,128)}), f32[512,512]{1,0:T(8,128)}) %all-reduce.5.cloned.1.call-update) | async-done | bytes 1048592 | tf_op jit(solution)/shard_map/psum | solution.py:53
  595.7 1.5 add_multiply_fusion
  597.2 76.8 %all-gather.5.cloned.1.call-done = bf16[4608,512]{1,0:T(8,128)(2,1)} async-done(((bf16[288,512]{1,0:T(8,128)(2,1)}), bf16[4608,512]{1,0:T(8,128)(2,1)}) %all-gather.5.cloned.1.call-update) | async-done | bytes 4718608 | tf_op jit(solution)/shard_map/all_gather | solution.py:33
  674.0 5.2 convolution_convert_fusion
  679.1 85.3 %reduce-scatter.7.cloned.1.call-done = f32[288,288]{1,0:T(8,128)} async-done(((f32[4608,288]{1,0:T(8,128)}), f32[288,288]{1,0:T(8,128)}) %reduce-scatter.7.cloned.1.call-update) | async-done | bytes 331792
  764.5 1.2 copy.13
  765.7 0.8 multiply_add_fusion
  766.5 80.1 %all-gather.9.cloned.1.call-done = f32[4608,512]{1,0:T(8,128)} async-done(((f32[288,512]{1,0:T(8,128)}), f32[4608,512]{1,0:T(8,128)}) %all-gather.9.cloned.1.call-update) | async-done | bytes 9437200 | tf_op jit(solution)/shard_map/all_gather | solution.py:62
  846.6 4.8 reduce_sum.9
  851.4 0.1 dynamic-slice_convert_fusion
  851.5 0.7 copy.11
  (19 shorter events, 0.1 us)
Async XLA Ops:
  7.2 330.0 %copy-start = (f32[512,512]{1,0:T(8,128)S(1)}, f32[512,512]{1,0:T(8,128)}, u32[]{:S(2)}) copy-start(f32[512,512]{1,0:T(8,128)} %param.13) | copy-start | bytes 3145732
  7.2 8.2 copy-start.2
  7.2 9.6 %copy-start.7 = (bf16[1,16,16,512]{3,2,1,0:T(8,128)(2,1)S(1)}, bf16[1,16,16,512]{3,2,1,0:T(8,128)(2,1)}, u32[]{:S(2)}) copy-start(bf16[1,16,16,512]{3,2,1,0:T(8,128)(2,1)} %param.8) | copy-start | bytes 786436
  7.2 130.8 %reduce-scatter.5.cloned.1.call-start = ((), (), s32[]{:S(2)}) async-start(), calls=%async_computation.5 | async-start | bytes 10027008 | tf_op jit(solution)/shard_map/reduce_scatter | solution.py:39
  15.5 1.4 copy-start.6
  21.9 178.4 %all-gather.7.cloned.1.call-start = ((), (), s32[]{:S(2)}) async-start(), calls=%async_computation.3 | async-start | bytes 4456448 | tf_op jit(solution)/shard_map/all_gather | solution.py:37
  22.7 314.5 %all-reduce.7.cloned.1.call-start = ((), (), s32[]{:S(2)}) async-start(), calls=%async_computation.6 | async-start | bytes 1179648 | tf_op jit(solution)/shard_map/psum | solution.py:50
  138.0 457.7 %all-reduce.5.cloned.1.call-start = ((), (), s32[]{:S(2)}) async-start(), calls=%async_computation.4 | async-start | bytes 2097152 | tf_op jit(solution)/shard_map/psum | solution.py:53
  139.4 534.6 %all-gather.5.cloned.1.call-start = ((), (), s32[]{:S(2)}) async-start(), calls=%async_computation.2 | async-start | bytes 5013504 | tf_op jit(solution)/shard_map/all_gather | solution.py:33
  140.0 624.5 %reduce-scatter.7.cloned.1.call-start = ((), (), s32[]{:S(2)}) async-start(), calls=%async_computation.8 | async-start | bytes 7520256
  200.3 5.6 copy-start.1
  262.4 77.1 %copy-start.3 = (f32[288,288]{1,0:T(8,128)S(1)}, f32[288,288]{1,0:T(8,128)}, u32[]{:S(2)}) copy-start(f32[288,288]{1,0:T(8,128)} %param.12) | copy-start | bytes 995332
  262.4 333.3 %copy-start.5 = (f32[32,512]{1,0:T(8,128)S(1)}, f32[32,512]{1,0:T(8,128)}, u32[]{:S(2)}) copy-start(f32[32,512]{1,0:T(8,128)} %param.11) | copy-start | bytes 196612
  262.4 584.3 %all-gather.9.cloned.1.call-start = ((), (), s32[]{:S(2)}) async-start(), calls=%async_computation.7 | async-start | bytes 10027008 | tf_op jit(solution)/shard_map/all_gather | solution.py:62
  674.0 91.7 %copy-start.4 = (f32[288,288]{1,0:T(8,128)S(1)}, f32[288,288]{1,0:T(8,128)}, u32[]{:S(2)}) copy-start(f32[288,288]{1,0:T(8,128)} %param.10) | copy-start | bytes 995332
Sparse Core Ops, SparseCore 0:
  22.1 115.8 reduce-scatter.4
  141.1 59.1 all-gather.6
  203.1 134.0 all-reduce.6
  342.5 253.1 all-reduce.4
  597.5 76.4 all-gather.4
  676.6 87.8 reduce-scatter.6
  767.2 79.3 all-gather.8
